TPU v7x, 32 devices: a whole 2x2x4 slice. The times are simulated.
32 devices in a mesh: rows: 8 (over y, x, core), feat: 4 (over z).
Axes of the slice: x: 2, y: 2, z: 4, core: 2. Of those that a mesh axis runs over, the one named last changes fastest.
Arguments:
- features: bfloat16 [16384, 512], P(('rows', 'feat')), may hold values from -6 to 6
- weight: bfloat16 [512, 512], replicated, may hold values from -0.25 to 0.25
- layer_bias: float32 [512], replicated, may hold values from -3 to 3
- block_cols: int32 [128, 6], P(('rows', 'feat')), may hold values from 0 to 127, as said below
- neighbours: int32 [16384, 30], P(('rows', 'feat')), may hold values from 0 to 767
- row_counts: int32 [16384], P(('rows', 'feat')), may hold values from 1 to 30
- out_grad: bfloat16 [16384, 512], P(('rows', 'feat')), may hold values from -6 to 6
Outputs:
- hidden: bfloat16 [16384, 512], P(('rows', 'feat'))
- input_grad: bfloat16 [16384, 512], P(('rows', 'feat'))
- weight_grad: float32 [512, 512], P('rows')
- bias_grad: float32 [512], P('rows')
Inputs may be any that keep to these rules, and one draw needn't show every extreme that they name: `block_cols`: block row t is node rows 128 * t to 128 * t + 127. With g = (t // 4) * 4: slot 0 is t itself, slot 1 lies in tiles g - 4 to g - 1, slot 2 in tiles g + 4 to g + 2 * 4 - 1, and every slot in tiles g - 4 to g + 2 * 4 - 1, all taken modulo 128. `neighbours`: entries at positions row_counts or later are unused.
All inputs are finite; a program needn't handle non-finite values.
Results may differ from a plain program's by a relative error of at most 0.0095.
Values may be sent and summed in bfloat16 or wider, within the bound.
A program may use at most 64 MiB of HBM per device.

v0:
```python
import math

import jax
import jax.numpy as jnp
from jax import lax
from jax.sharding import PartitionSpec as P

precise = lax.Precision.HIGHEST


def extended(array, sides, width):
    for axis, dim in sides:
        peers, length = (lax.axis_size(axis), array.shape[dim])
        up = [(i, (i + 1) % peers) for i in range(peers)]
        down = [(j, i) for i, j in up]
        last = lax.slice_in_dim(array, length - width, length, axis=dim)
        initial = lax.slice_in_dim(array, 0, width, axis=dim)
        before = lax.ppermute(last, axis, up)
        after = lax.ppermute(initial, axis, down)
        array = jnp.concatenate([before, array, after], axis=dim)
    return array


def from_behind(block, axis, distance):
    devices = range(lax.axis_size(axis))
    route = [((i - distance) % len(devices), i) for i in devices]
    return lax.ppermute(block, axis, route)


def strip_counts(neighbours, row_counts, strip_width):
    columns = jnp.arange(strip_width, dtype=jnp.int32)
    slot_ids = jnp.arange(neighbours.shape[1], dtype=jnp.int32)
    live_slot = slot_ids[None, :] < row_counts[:, None]
    matches = (neighbours[:, :, None] == columns[None, None, :]) & live_slot[:, :, None]
    return jnp.sum(matches.astype(jnp.int32), axis=1).astype(jnp.bfloat16)


def local(features, weight, layer_bias, block_cols, neighbours, row_counts, out_grad):
    rows_dev = features.shape[0]
    feat_width = features.shape[1]
    tile_count = block_cols.shape[0]
    tile_rows = rows_dev // tile_count
    slot_count = block_cols.shape[1]
    devices = lax.axis_size("rows") * lax.axis_size("feat")
    all_tiles = tile_count * devices
    normaliser = 1.0 / math.sqrt(rows_dev * devices)
    own_start = lax.axis_index(("rows", "feat")) * tile_count
    window_start = own_start - tile_count
    local_slot = jnp.mod(block_cols - window_start, all_tiles)
    inverse_root = lax.rsqrt(1.0 + row_counts.astype(jnp.float32))[:, None]
    projected = jnp.dot(features, weight, preferred_element_type=jnp.float32)
    proj_scaled = (projected * inverse_root).astype(jnp.bfloat16)
    window = extended(proj_scaled, ((("rows", "feat"), 0),), rows_dev)
    window_tiles = window.reshape(3 * tile_count, tile_rows, feat_width)
    strips = []
    aggregated = []
    for tile_index in range(tile_count):
        lower_row = tile_index * tile_rows
        count_strip = strip_counts(
            neighbours[lower_row : lower_row + tile_rows],
            row_counts[lower_row : lower_row + tile_rows],
            slot_count * tile_rows,
        )
        sources = jnp.take(window_tiles, local_slot[tile_index], axis=0).reshape(
            slot_count * tile_rows, feat_width
        )
        aggregated.append(jnp.dot(count_strip, sources, preferred_element_type=jnp.float32))
        strips.append(count_strip)
    summed = jnp.concatenate(aggregated, axis=0)
    pre_activation = inverse_root * (summed + proj_scaled.astype(jnp.float32)) + layer_bias[None, :]
    sigmoid_gate = jax.nn.sigmoid(pre_activation)
    hidden = (pre_activation * sigmoid_gate).astype(jnp.bfloat16)
    grad_pre = (
        out_grad.astype(jnp.float32) * sigmoid_gate * (1.0 + pre_activation * (1.0 - sigmoid_gate))
    )
    grad_scaled = (grad_pre * inverse_root).astype(jnp.bfloat16)
    pieces = []
    for tile_index in range(tile_count):
        lower_row = tile_index * tile_rows
        pieces.append(
            lax.dot_general(
                strips[tile_index],
                grad_scaled[lower_row : lower_row + tile_rows],
                (((0,), (0,)), ((), ())),
                preferred_element_type=jnp.float32,
            )
        )
    spread = jnp.stack(pieces).reshape(tile_count * slot_count, tile_rows * feat_width)
    window_ids = jnp.arange(3 * tile_count, dtype=jnp.int32)
    owner_table = (local_slot.reshape(-1)[None, :] == window_ids[:, None]).astype(jnp.float32)
    returned = jnp.dot(owner_table, spread, precision=precise).reshape(3 * rows_dev, feat_width)
    left_part = returned[:rows_dev]
    own_part = returned[rows_dev : 2 * rows_dev]
    right_part = returned[2 * rows_dev :]
    from_right = from_behind(left_part, ("rows", "feat"), -1)
    from_left = from_behind(right_part, ("rows", "feat"), 1)
    incoming = own_part + from_right + from_left
    grad_proj = (inverse_root * (incoming + grad_scaled.astype(jnp.float32))).astype(jnp.bfloat16)
    input_grad = lax.dot_general(
        grad_proj, weight, (((1,), (1,)), ((), ())), preferred_element_type=jnp.float32
    ).astype(jnp.bfloat16)
    local_weight = lax.dot_general(
        features, grad_proj, (((0,), (0,)), ((), ())), preferred_element_type=jnp.float32
    )
    local_bias = jnp.sum(grad_pre, axis=0)
    total_weight, total_bias = lax.psum((local_weight, local_bias), ("rows", "feat"))
    row_share = feat_width // lax.axis_size("rows")
    row_start = lax.axis_index("rows") * row_share
    part_weight = lax.dynamic_slice_in_dim(total_weight, row_start, row_share, 0)
    part_bias = lax.dynamic_slice_in_dim(total_bias, row_start, row_share, 0)
    return (hidden, input_grad, part_weight * normaliser, part_bias * normaliser)


def solution(mesh):
    in_specs = (
        P(("rows", "feat"), None),
        P(),
        P(),
        P(("rows", "feat"), None),
        P(("rows", "feat"), None),
        P(("rows", "feat")),
        P(("rows", "feat"), None),
    )
    out_specs = (P(("rows", "feat"), None), P(("rows", "feat"), None), P("rows", None), P("rows"))
    return jax.shard_map(local, mesh=mesh, in_specs=in_specs, out_specs=out_specs, check_vma=False)
```

profile of v0, /device:TPU:0, one launch (start us, length us, event | category | flops | bytes accessed | tf_op | source)
XLA Modules:
  0.0 266.1 jit_solution(10925588107084807310)
XLA Ops:
  8.2 1.5 fusion.4
  9.7 6.4 %collective-permute-start.1 = (bf16[512,512]{1,0:T(8,128)(2,1)S(1)}, bf16[512,512]{1,0:T(8,128)(2,1)S(1)}, u32[]{:S(2)}, u32[]{:S(2)}) collective-permute-start(bf16[512,512]{1,0:T(8,128)(2,1)S(1)} %fusion.4), channel_id=1, source_target_pairs={{1,0},{2,1},{3,2},{4,3},{5,4},{6,5},{7,6},{8,7},{9,8},{10,9},{11,1... | collective-permute-start | bytes 1572872 | tf_op jit(solution)/shard_map/ppermute | solution.py:19
  18.7 4.6 %convert_reduce_fusion.2 = (s32[128,768]{1,0:T(8,128)S(1)}, s32[128,768]{1,0:T(8,128)S(1)}) fusion(s32[128,30]{0,1:T(8,128)S(1)} %get-tuple-element.28, pred[128,30]{0,1:T(8,128)(4,1)S(1)} %iota_compare_fusion.6, pred[128,30]{0,1:T(8,128)(4,1)S(1)} %iota_compare_fusion.7, s32[128,30]{0,1:T(8,128)S(1)} %get-tuple-element.27), kind=kLoop, calls=%fused_computation.8 | loop fusion | flops 23396352 | bytes 824832 | tf_op jit(solution)/shard_map/reduce_sum | solution.py:35
  23.3 5.3 %convert_reduce_fusion = (s32[128,768]{1,0:T(8,128)}, s32[128,768]{1,0:T(8,128)S(1)}) fusion(s32[128,30]{0,1:T(8,128)S(1)} %get-tuple-element.29, pred[128,30]{0,1:T(8,128)(4,1)S(1)} %iota_compare_fusion.4, pred[128,30]{0,1:T(8,128)(4,1)S(1)} %iota_compare_fusion.5, s32[128,30]{0,1:T(8,128)S(1)} %get-tuple-element.30), kind=kLoop, calls=%fused_computation.4 | loop fusion | flops 23396352 | bytes 824832 | tf_op jit(solution)/shard_map/reduce_sum | solution.py:35
  29.4 9.6 %collective-permute-done = bf16[512,512]{1,0:T(8,128)(2,1)} collective-permute-done((bf16[512,512]{1,0:T(8,128)(2,1)S(1)}, bf16[512,512]{1,0:T(8,128)(2,1)}, u32[]{:S(2)}, u32[]{:S(2)}) %collective-permute-start) | collective-permute-done | bytes 524320 | tf_op jit(solution)/shard_map/ppermute | solution.py:18
  40.4 1.5 gather_fusion.3
  42.0 1.5 gather_fusion.2
  43.5 1.5 gather_fusion.1
  45.0 1.5 gather_fusion
  46.5 1.7 broadcast_select_fusion
  53.2 2.9 %pad_maximum_fusion = f32[4,768,512]{2,1,0:T(8,128)} fusion(f32[1,768,512]{2,1,0:T(8,128)S(1)} %convolution_bitcast_fusion, f32[1,768,512]{2,1,0:T(8,128)S(1)} %convolution_bitcast_fusion.1, f32[1,768,512]{2,1,0:T(8,128)S(1)} %convolution_bitcast_fusion.2, f32[1,768,512]{2,1,0:T(8,128)S(1)} %convolution_bitcast_fusion.3), kind=kLoop, calls=%fused_computation.16 | loop fusion | flops 4718592 | bytes 12582912 | tf_op jit(solution)/shard_map/stack | solution.py:88
  56.1 6.8 %reshape.131 = f32[24,65536]{1,0:T(8,128)} reshape(f32[4,768,512]{2,1,0:T(8,128)} %pad_maximum_fusion) | data formatting | bytes 12582912 | tf_op jit(solution)/shard_map/reshape | solution.py:88
  62.9 4.6 %fusion.23 = f32[12,65536]{1,0:T(8,128)S(1)} fusion(f32[24,65536]{1,0:T(8,128)} %reshape.131, s32[24]{0:T(128)S(1)} %eq.81), kind=kOutput, calls=%fused_computation.60 | convolution fusion | flops 226492704 | bytes 9437280 | tf_op jit(solution)/shard_map/dot_general | solution.py:91
  67.6 1.8 fusion.27
  69.4 2.9 %slice.85 = f32[512,512]{1,0:T(8,128)} reshape(f32[4,65536]{1,0:T(4,128)} %get-tuple-element.23) | data formatting | bytes 2097152 | tf_op jit(solution)/shard_map/slice | solution.py:92
  72.3 3.0 %slice.87 = f32[512,512]{1,0:T(8,128)} reshape(f32[4,65536]{1,0:T(4,128)} %get-tuple-element.24) | data formatting | bytes 2097152 | tf_op jit(solution)/shard_map/slice | solution.py:94
  76.7 3.9 %collective-permute-start.2 = (f32[512,512]{1,0:T(8,128)}, f32[512,512]{1,0:T(8,128)}, u32[]{:S(2)}, u32[]{:S(2)}) collective-permute-start(f32[512,512]{1,0:T(8,128)} %slice.85), channel_id=1, source_target_pairs={{1,0},{2,1},{3,2},{4,3},{5,4},{6,5},{7,6},{8,7},{9,8},{10,9},{11,1... | collective-permute-start | bytes 3145736 | tf_op jit(solution)/shard_map/ppermute | solution.py:27
  80.6 1.7 slice.83
  82.3 22.3 %collective-permute-done.3 = f32[512,512]{1,0:T(8,128)} collective-permute-done((f32[512,512]{1,0:T(8,128)}, f32[512,512]{1,0:T(8,128)}, u32[]{:S(2)}, u32[]{:S(2)}) %collective-permute-start.3) | collective-permute-done | bytes 1048608 | tf_op jit(solution)/shard_map/ppermute | solution.py:27
  104.6 17.9 %collective-permute-done.2 = f32[512,512]{1,0:T(8,128)} collective-permute-done((f32[512,512]{1,0:T(8,128)}, f32[512,512]{1,0:T(8,128)}, u32[]{:S(2)}, u32[]{:S(2)}) %collective-permute-start.2) | collective-permute-done | bytes 1048608 | tf_op jit(solution)/shard_map/ppermute | solution.py:27
  122.5 2.1 multiply_convert_fusion
  124.6 1.5 convolution_bitcast_fusion.4
  126.1 41.0 %psum.15 = f32[512]{0:T(512)S(1)} all-reduce(f32[512]{0:T(512)S(1)} %get-tuple-element.13), channel_id=1, replica_groups=mesh['rows'=8,'feat'=4] {'rows','feat'}, use_global_device_ids=true, to_apply=%region_6.8 | all-reduce | flops 512 | bytes 4096 | tf_op jit(solution)/shard_map/psum | solution.py:106
  169.0 88.5 %all-reduce.2.cloned.1.call-done = f32[512,512]{0,1:T(8,128)} async-done(((f32[512,512]{0,1:T(8,128)}), f32[512,512]{0,1:T(8,128)}) %all-reduce.2.cloned.1.call-update) | async-done | bytes 1048592 | tf_op jit(solution)/shard_map/psum | solution.py:106
  (55 shorter events, 15.8 us)
Async XLA Ops:
  7.2 1.1 copy-start
  7.2 250.3 %all-reduce.2.cloned.1.call-start = ((), (), s32[]{:S(2)}) async-start(), calls=%async_computation | async-start | bytes 2097152 | tf_op jit(solution)/shard_map/psum | solution.py:106
  9.7 18.9 %copy-start.4 = (bf16[512,512]{1,0:T(8,128)(2,1)}, bf16[512,512]{1,0:T(8,128)(2,1)S(1)}, u32[]{:S(2)}) copy-start(bf16[512,512]{1,0:T(8,128)(2,1)S(1)} %fusion.4) | copy-start | bytes 1572868
  9.7 18.9 %collective-permute-start.1 = (bf16[512,512]{1,0:T(8,128)(2,1)S(1)}, bf16[512,512]{1,0:T(8,128)(2,1)S(1)}, u32[]{:S(2)}, u32[]{:S(2)}) collective-permute-start(bf16[512,512]{1,0:T(8,128)(2,1)S(1)} %fusion.4), channel_id=1, source_target_pairs={{1,0},{2,1},{3,2},{4,3},{5,4},{6,5},{7,6},{8,7},{9,8},{10,9},{11,1... | collective-permute-start | bytes 1572872 | tf_op jit(solution)/shard_map/ppermute | solution.py:19
  16.2 22.8 %collective-permute-start = (bf16[512,512]{1,0:T(8,128)(2,1)S(1)}, bf16[512,512]{1,0:T(8,128)(2,1)}, u32[]{:S(2)}, u32[]{:S(2)}) collective-permute-start(bf16[512,512]{1,0:T(8,128)(2,1)S(1)} %fusion.4), channel_id=1, source_target_pairs={{0,1},{1,2},{2,3},{3,4},{4,5},{5,6},{6,7},{7,8},{8,9},{9,10},{10,1... | collective-permute-start | bytes 1572872 | tf_op jit(solution)/shard_map/ppermute | solution.py:18
  28.6 0.8 copy-start.8
  46.5 1.7 copy-start.1
  46.5 2.3 copy-start.2
  46.5 2.3 copy-start.3
  48.8 1.0 copy-start.5
  48.8 1.2 copy-start.7
  48.8 1.2 copy-start.9
  75.2 29.4 %collective-permute-start.3 = (f32[512,512]{1,0:T(8,128)}, f32[512,512]{1,0:T(8,128)}, u32[]{:S(2)}, u32[]{:S(2)}) collective-permute-start(f32[512,512]{1,0:T(8,128)} %slice.87), channel_id=1, source_target_pairs={{31,0},{0,1},{1,2},{2,3},{3,4},{4,5},{5,6},{6,7},{7,8},{8,9},{9,10... | collective-permute-start | bytes 3145736 | tf_op jit(solution)/shard_map/ppermute | solution.py:27
  76.7 45.8 %collective-permute-start.2 = (f32[512,512]{1,0:T(8,128)}, f32[512,512]{1,0:T(8,128)}, u32[]{:S(2)}, u32[]{:S(2)}) collective-permute-start(f32[512,512]{1,0:T(8,128)} %slice.85), channel_id=1, source_target_pairs={{1,0},{2,1},{3,2},{4,3},{5,4},{6,5},{7,6},{8,7},{9,8},{10,9},{11,1... | collective-permute-start | bytes 3145736 | tf_op jit(solution)/shard_map/ppermute | solution.py:27
  82.3 85.4 %copy-start.6 = (bf16[512,512]{1,0:T(8,128)(2,1)S(1)}, bf16[512,512]{1,0:T(8,128)(2,1)}, u32[]{:S(2)}) copy-start(bf16[512,512]{1,0:T(8,128)(2,1)} %param.10) | copy-start | bytes 1572868
Sparse Core Ops, SparseCore 0:
  126.2 131.1 all-reduce.1
where the time goes:
time: 267 us; the launch traced here: 266 us
  waiting for transfers between devices  138 us (52%)
  blocking collectives  41 us (15%)
  local copies, waits for them, and re-layouts  26.2 us (10%)
  other arithmetic  23 us (9%)
  between operations  14.3 us (5%)
  starting transfers between devices  11.8 us (4%)
  matrix products  11.5 us (4%)
    psum x1, waiting for transfers between devices, local(): lax.psum((local_weight, local_bias), ('rows', 'feat'))  88.5 us
    psum x1, blocking collectives, local(): lax.psum((local_weight, local_bias), ('rows', 'feat'))  41 us
    ppermute x2, waiting for transfers between devices, from_behind(): return lax.ppermute(block, axis, route)  40.2 us
    reduce_sum x2, other arithmetic, strip_counts(): return jnp.sum(matches.astype(jnp.int32), axis=1).astype(jnp.bfloat16)  9.9 us
    ppermute x1, waiting for transfers between devices, extended(): before = lax.ppermute(last, axis, up)  9.6 us
    reshape x1, local copies, waits for them, and re-layouts, local(): jnp.stack(pieces).reshape(tile_count * slot_count, tile_rows * feat_width)  6.84 us
    ppermute x1, starting transfers between devices, extended(): after = lax.ppermute(initial, axis, down)  6.43 us
    gather x4, local copies, waits for them, and re-layouts, local(): jnp.take(window_tiles, local_slot[tile_index], axis=0)  6.05 us
  transfers between devices with their start and end apart: 5, of which 4 were waited for; matrix products, arithmetic and copies ran while one was open for 6% of the time, Pallas kernels for 0%

commit v1 on v0

v1 whole, which is shorter than its diff:
```python
import functools
import math

import jax
import jax.numpy as jnp
from jax import lax
from jax.experimental import pallas as pl
from jax.experimental.pallas import tpu as pltpu
from jax.sharding import PartitionSpec as P

LANES = 128
GROUP = 16
f32 = jnp.float32
bf16 = jnp.bfloat16


def matmul(a, b):
    return jnp.dot(a, b, preferred_element_type=f32)


def kernel(
    rows_n, feat_n, scale,
    features, weight, bias, out_grad, keys, inverse_root,
    hidden, input_grad, weight_grad, bias_grad,
    window, adj, adj_t, features_t, part_out, part_in, own, grad_proj,
    wsend, wrecv, zbuf, bsend, brecv, bz,
    fwd_send, fwd_recv, bwd_send, bwd_recv, ws_sem, wr_sem, zs_sem, zr_sem,
    bs_sem, br_sem, bzs_sem, bzr_sem,
):
    n = features.shape[0]
    chunks = window.shape[0]
    share = weight_grad.shape[0]
    r = lax.axis_index("rows")
    z = lax.axis_index("feat")
    count = rows_n * feat_n
    me = r * feat_n + z
    prev = lax.rem(me + count - 1, count)
    succ = lax.rem(me + 1, count)
    sides = (
        {"rows": lax.div(prev, feat_n), "feat": lax.rem(prev, feat_n)},
        {"rows": lax.div(succ, feat_n), "feat": lax.rem(succ, feat_n)},
    )

    def row_peer(d):
        return {"rows": lax.rem(r + d, rows_n), "feat": z}

    def feat_peer(d):
        return {"rows": r, "feat": lax.rem(z + d, feat_n)}

    def remote(src, dst, send, recv, device):
        return pltpu.make_async_remote_copy(
            src_ref=src, dst_ref=dst, send_sem=send, recv_sem=recv,
            device_id=device, device_id_type=pl.DeviceIdType.MESH,
        )

    def each(size, act):
        def body(d, carry):
            act(d)
            return carry
        lax.fori_loop(1, size, body, 0)

    def cols(c):
        return pl.ds(c * LANES, LANES)

    def fwd(side, c):
        place = pl.ds(2 * n if side == 0 else 0, n)
        return remote(
            window.at[c, pl.ds(n, n)], window.at[c, place],
            fwd_send.at[side, c], fwd_recv.at[side, c], sides[side],
        )

    def bwd(side, c):
        return remote(
            part_out.at[side, c], part_in.at[side, c],
            bwd_send.at[side, c], bwd_recv.at[side, c], sides[side],
        )

    def wcopy(c, d):
        peer = row_peer(d)
        start = pl.multiple_of(peer["rows"] * share, share)
        return remote(
            wsend.at[c, pl.ds(start, share)], wrecv.at[c, d], ws_sem.at[c, d], wr_sem.at[c, d], peer
        )

    def zcopy(c, d):
        return remote(zbuf.at[c, z], zbuf.at[c, z], zs_sem.at[c, d], zr_sem.at[c, d], feat_peer(d))

    def bcopy(d):
        return remote(bsend, brecv.at[d], bs_sem.at[d], br_sem.at[d], row_peer(d))

    def bzcopy(d):
        return remote(bz.at[z], bz.at[z], bzs_sem.at[d], bzr_sem.at[d], feat_peer(d))

    barrier = pltpu.get_barrier_semaphore()

    def greet(device):
        pl.semaphore_signal(
            barrier, inc=1, device_id=device, device_id_type=pl.DeviceIdType.MESH
        )

    greet(sides[0])
    greet(sides[1])
    each(rows_n, lambda d: greet(row_peer(d)))
    each(feat_n, lambda d: greet(feat_peer(d)))

    for c in range(chunks):
        product = matmul(features[...], weight[:, cols(c)])
        window[c, pl.ds(n, n), :] = (product * inverse_root[...]).astype(bf16)
        if c == 0:
            pl.semaphore_wait(barrier, rows_n + feat_n)
        fwd(0, c).start()
        fwd(1, c).start()

    features_t[...] = features[...].T
    columns = lax.broadcasted_iota(jnp.int32, (GROUP, 3 * n), 1)

    def fill(g, carry):
        at = pl.ds(pl.multiple_of(g * GROUP, GROUP), GROUP)
        mine = keys[at, :]
        total = jnp.zeros((GROUP, 3 * n), jnp.int32)
        for k in range(keys.shape[1]):
            total = total + (mine[:, k : k + 1] == columns).astype(jnp.int32)
        adj[at, :] = total.astype(f32).astype(bf16)
        return carry

    lax.fori_loop(0, n // GROUP, fill, 0)
    for j in range(3):
        at = pl.ds(j * n, n)
        adj_t[at, :] = adj[:, at].T

    bsend[...] = jnp.zeros_like(bsend)
    for c in range(chunks):
        fwd(0, c).wait_recv()
        fwd(1, c).wait_recv()
        root = inverse_root[...]
        summed = matmul(adj[...], window[c]) + window[c, pl.ds(n, n), :].astype(f32)
        pre = root * summed + bias[:, cols(c)]
        gate = jax.nn.sigmoid(pre)
        grad_pre = out_grad[:, cols(c)].astype(f32) * gate * (1.0 + pre * (1.0 - gate))
        grad_scaled = (grad_pre * root).astype(bf16)
        part_out[0, c] = matmul(adj_t[pl.ds(0, n), :], grad_scaled).astype(bf16)
        bwd(0, c).start()
        part_out[1, c] = matmul(adj_t[pl.ds(2 * n, n), :], grad_scaled).astype(bf16)
        bwd(1, c).start()
        own[c] = matmul(adj_t[pl.ds(n, n), :], grad_scaled) + grad_scaled.astype(f32)
        hidden[:, cols(c)] = (pre * gate).astype(bf16)
        bsend[pl.ds(c, 1), :] = jnp.sum(grad_pre, axis=0, keepdims=True)
    each(rows_n, lambda d: bcopy(d).start())

    def share_rows(c):
        each(rows_n, lambda d: wcopy(c, d).wait_recv())
        total = wsend[c, pl.ds(pl.multiple_of(r * share, share), share), :].astype(f32)
        for d in range(1, rows_n):
            total = total + wrecv[c, d].astype(f32)
        zbuf[c, z] = total.astype(bf16)
        each(feat_n, lambda d: zcopy(c, d).start())

    for c in range(chunks):
        bwd(0, c).wait_recv()
        bwd(1, c).wait_recv()
        total = own[c] + part_in[0, c].astype(f32) + part_in[1, c].astype(f32)
        piece = (inverse_root[...] * total).astype(bf16)
        wsend[c] = matmul(features_t[...], piece).astype(bf16)
        each(rows_n, lambda d: wcopy(c, d).start())
        grad_proj[:, cols(c)] = piece
        if c == 0:
            each(rows_n, lambda d: bcopy(d).wait_recv())
            total_bias = bsend[...]
            for d in range(1, rows_n):
                total_bias = total_bias + brecv[d]
            bz[z] = total_bias
            each(feat_n, lambda d: bzcopy(d).start())
        else:
            share_rows(c - 1)

    input_grad[...] = lax.dot_general(
        grad_proj[...], weight[...], (((1,), (1,)), ((), ())), preferred_element_type=f32
    ).astype(bf16)
    share_rows(chunks - 1)
    each(feat_n, lambda d: bzcopy(d).wait_recv())
    total_bias = bz[0]
    for p in range(1, feat_n):
        total_bias = total_bias + bz[p]
    bias_grad[...] = total_bias * scale
    for c in range(chunks):
        each(feat_n, lambda d: zcopy(c, d).wait_recv())
        total = zbuf[c, 0].astype(f32)
        for p in range(1, feat_n):
            total = total + zbuf[c, p].astype(f32)
        weight_grad[:, cols(c)] = total * scale

    for c in range(chunks):
        for side in range(2):
            fwd(side, c).wait_send()
            bwd(side, c).wait_send()
        each(rows_n, lambda d: wcopy(c, d).wait_send())
        each(feat_n, lambda d: zcopy(c, d).wait_send())
    each(rows_n, lambda d: bcopy(d).wait_send())
    each(feat_n, lambda d: bzcopy(d).wait_send())


def local(features, weight, layer_bias, block_cols, neighbours, row_counts, out_grad):
    n, width = features.shape
    tile_count, slot_count = block_cols.shape
    tile_rows = n // tile_count
    slots = neighbours.shape[1]
    rows_n, feat_n = lax.axis_size("rows"), lax.axis_size("feat")
    devices = rows_n * feat_n
    scale = 1.0 / math.sqrt(n * devices)
    chunks = width // LANES
    share = width // rows_n

    window_start = (lax.axis_index(("rows", "feat")) - 1) * tile_count
    local_slot = jnp.mod(block_cols - window_start, tile_count * devices)
    used = jnp.arange(slots, dtype=jnp.int32)[None, :] < row_counts[:, None]
    named = neighbours // tile_rows
    base = jnp.zeros_like(neighbours)
    for s in range(slot_count):
        base = jnp.where(named == s, jnp.repeat(local_slot[:, s], tile_rows)[:, None], base)
    keys = jnp.where(used, base * tile_rows + neighbours % tile_rows, -1)
    inverse_root = lax.rsqrt(1.0 + row_counts.astype(f32))[:, None]

    vmem = pl.BlockSpec(memory_space=pltpu.VMEM)
    bias_rows = max(8, chunks)
    dma = pltpu.SemaphoreType.DMA
    hidden, input_grad, weight_grad, bias_grad = pl.pallas_call(
        functools.partial(kernel, rows_n, feat_n, scale),
        out_shape=(
            jax.ShapeDtypeStruct((n, width), bf16),
            jax.ShapeDtypeStruct((n, width), bf16),
            jax.ShapeDtypeStruct((share, width), f32),
            jax.ShapeDtypeStruct((bias_rows, LANES), f32),
        ),
        in_specs=[vmem] * 6,
        out_specs=(vmem,) * 4,
        scratch_shapes=[
            pltpu.VMEM((chunks, 3 * n, LANES), bf16),
            pltpu.VMEM((n, 3 * n), bf16),
            pltpu.VMEM((3 * n, n), bf16),
            pltpu.VMEM((width, n), bf16),
            pltpu.VMEM((2, chunks, n, LANES), bf16),
            pltpu.VMEM((2, chunks, n, LANES), bf16),
            pltpu.VMEM((chunks, n, LANES), f32),
            pltpu.VMEM((n, width), bf16),
            pltpu.VMEM((chunks, width, LANES), bf16),
            pltpu.VMEM((chunks, rows_n, share, LANES), bf16),
            pltpu.VMEM((chunks, feat_n, share, LANES), bf16),
            pltpu.VMEM((bias_rows, LANES), f32),
            pltpu.VMEM((rows_n, bias_rows, LANES), f32),
            pltpu.VMEM((feat_n, bias_rows, LANES), f32),
            dma((2, chunks)), dma((2, chunks)), dma((2, chunks)), dma((2, chunks)),
            dma((chunks, rows_n)), dma((chunks, rows_n)),
            dma((chunks, feat_n)), dma((chunks, feat_n)),
            dma((rows_n,)), dma((rows_n,)), dma((feat_n,)), dma((feat_n,)),
        ],
        compiler_params=pltpu.CompilerParams(
            collective_id=0, has_side_effects=True, vmem_limit_bytes=48 * 2**20
        ),
        cost_estimate=pl.CostEstimate(
            flops=18 * n * width * width, bytes_accessed=12 * n * width, transcendentals=n * width
        ),
    )(features, weight, layer_bias[None, :], out_grad, keys, inverse_root)
    part_bias = lax.dynamic_slice_in_dim(
        bias_grad.reshape(-1), lax.axis_index("rows") * share, share, 0
    )
    return hidden, input_grad, weight_grad, part_bias


def solution(mesh):
    in_specs = (
        P(("rows", "feat"), None),
        P(),
        P(),
        P(("rows", "feat"), None),
        P(("rows", "feat"), None),
        P(("rows", "feat")),
        P(("rows", "feat"), None),
    )
    out_specs = (P(("rows", "feat"), None), P(("rows", "feat"), None), P("rows", None), P("rows"))
    return jax.shard_map(local, mesh=mesh, in_specs=in_specs, out_specs=out_specs, check_vma=False)
```

time: 267 us -> 70.4 us (0.26)
  waiting for transfers between devices: 138 us -> 0 us
  Pallas kernels: 0 us -> 62 us
  blocking collectives: 41 us -> 0 us
  other arithmetic: 23 us -> 0.7 us
  local copies, waits for them, and re-layouts: 26.2 us -> 6.69 us
  between operations: 14.3 us -> 0.72 us
  starting transfers between devices: 11.8 us -> 0 us
  matrix products: 11.5 us -> 0 us
    psum x1 -> x0, waiting for transfers between devices: 88.5 us -> none  [local(): lax.psum((local_weight, local_bias), ('rows', 'feat'))]
    pallas_call x0 -> x1, Pallas kernels: none -> 62 us  [local(): pl.pallas_call(functools.partial(kernel, rows_n, feat_n, scale), out_shap...]
    ppermute x4 -> x0, waiting for transfers between devices: 49.8 us -> none  [the longest x2 40.2 us: from_behind(): return lax.ppermute(block, axis, route)]
    psum x1 -> x0, blocking collectives: 41 us -> none  [local(): lax.psum((local_weight, local_bias), ('rows', 'feat'))]
    ppermute x4 -> x0, starting transfers between devices: 11.8 us -> none  [the longest x1 6.43 us: extended(): after = lax.ppermute(initial, axis, down)]
    dot_general x12 -> x0, matrix products: 11.5 us -> none  [the longest x1 4.64 us: local(): jnp.dot(owner_table, spread, precision=precise)]
    reduce_sum x3 -> x0, other arithmetic: 11.3 us -> none  [the longest x2 9.9 us: strip_counts(): return jnp.sum(matches.astype(jnp.int32), axis=1).astype(jnp.bfloat16)]
    slice x6 -> x1, local copies, waits for them, and re-layouts: 11 us -> 0.25 us  [local(): local_slot[:, s]]
  transfers between devices with their start and end apart: 5 -> 0, of which waited for: 4 -> 0; matrix products, arithmetic and copies ran while one was open for 6% -> 0% of each run, Pallas kernels for 0% -> 0%
where the time goes in v1:
time: 70.4 us; the launch traced here: 70.1 us
  Pallas kernels  62 us (88%)
  local copies, waits for them, and re-layouts  6.69 us (10%)
  between operations  0.72 us (1%)
    pallas_call x1, Pallas kernels, local(): pl.pallas_call(functools.partial(kernel, rows_n, feat_n, scale), out_shap...  62 us
    unnamed x18, local copies, waits for them, and re-layouts  5.49 us

profile of v1, /device:TPU:0, one launch (start us, length us, event | category | flops | bytes accessed | tf_op | source)
XLA Modules:
  0.0 70.1 jit_solution(17021971371989369000)
XLA Ops:
  0.6 0.0 copy-start.6
  0.6 0.7 copy-done.6
  1.3 0.3 slice_reduce_fusion.5
  1.6 0.0 copy-start.5
  1.6 0.7 copy-done.5
  2.3 0.1 broadcast_bitcast_fusion.4
  2.3 0.1 broadcast_bitcast_fusion
  2.4 0.1 broadcast_bitcast_fusion.2
  2.5 0.0 copy-start.4
  2.5 0.0 copy-start
  2.5 0.2 copy.19.inverse_root
  2.7 0.7 copy-done.4
  3.3 0.1 copy.15
  3.5 0.0 copy-start.3
  3.5 0.7 fusion.1.keys
  4.2 0.0 copy-done
  4.2 0.0 copy-done.1
  4.2 0.0 copy-done.3
  4.2 1.0 %copy-done.2 = bf16[512,512]{1,0:T(8,128)(2,1)S(1)} copy-done((bf16[512,512]{1,0:T(8,128)(2,1)S(1)}, bf16[512,512]{1,0:T(8,128)(2,1)}, u32[]{:S(2)}) %copy-start.2) | copy-done | bytes 524312
  5.3 62.0 %shard_map.102 = (bf16[512,512]{1,0:T(8,128)(2,1)S(1)}, bf16[512,512]{1,0:T(8,128)(2,1)S(1)}, f32[64,512]{1,0:T(8,128)S(1)}, f32[8,128]{1,0:T(8,128)S(1)}) custom-call(bf16[512,512]{1,0:T(8,128)(2,1)S(1)} %copy-done, bf16[512,512]{1,0:T(8,128)(2,1)S(1)} %copy-done.1, f32[1,512]{1,0:T(1,128)S(1)} %bitcast.15, bf16[512,512]{1,0:T(8,128)(2,1)S(1)} %copy-done.2, ...), custom_call_target="tpu_custom_call" | custom-call | flops 2415919104 | bytes 3145728 | tf_op jit(solution)/shard_map/pallas_call | solution.py:226
  67.3 0.6 dynamic_slice.3
  67.9 0.8 %copy.23 = bf16[512,512]{1,0:T(8,128)(2,1)} copy(bf16[512,512]{1,0:T(8,128)(2,1)S(1)} %get-tuple-element.28) | data formatting | bytes 1048576
  68.7 0.8 %copy.24 = bf16[512,512]{1,0:T(8,128)(2,1)} copy(bf16[512,512]{1,0:T(8,128)(2,1)S(1)} %get-tuple-element.29) | data formatting | bytes 1048576
  69.5 0.7 copy.25
  (4 shorter events, 0.0 us)
Async XLA Ops:
  0.6 0.7 copy-start.6
  1.6 0.7 copy-start.5
  2.5 0.8 %copy-start.4 = (s32[512,30]{0,1:T(8,128)S(1)}, s32[512,30]{0,1:T(8,128)}, u32[]{:S(2)}) copy-start(s32[512,30]{0,1:T(8,128)} %param.11) | copy-start | bytes 184324
  2.5 1.7 %copy-start = (bf16[512,512]{1,0:T(8,128)(2,1)S(1)}, bf16[512,512]{1,0:T(8,128)(2,1)}, u32[]{:S(2)}) copy-start(bf16[512,512]{1,0:T(8,128)(2,1)} %features.1) | copy-start | bytes 1572868
  2.5 1.7 %copy-start.1 = (bf16[512,512]{1,0:T(8,128)(2,1)S(1)}, bf16[512,512]{1,0:T(8,128)(2,1)}, u32[]{:S(2)}) copy-start(bf16[512,512]{1,0:T(8,128)(2,1)} %weight.1) | copy-start | bytes 1572868
  3.5 0.8 %copy-start.3 = (f32[512]{0:T(512)S(1)}, f32[512]{0:T(512)}, u32[]{:S(2)}) copy-start(f32[512]{0:T(512)} %param.9) | copy-start | bytes 6148
  4.2 1.0 %copy-start.2 = (bf16[512,512]{1,0:T(8,128)(2,1)S(1)}, bf16[512,512]{1,0:T(8,128)(2,1)}, u32[]{:S(2)}) copy-start(bf16[512,512]{1,0:T(8,128)(2,1)} %out_grad.1) | copy-start | bytes 1572868

commit v2 on v1

--- a/solution.py
+++ b/solution.py
@@ -9,7 +9,6 @@
 from jax.sharding import PartitionSpec as P
 
 LANES = 128
-GROUP = 16
 f32 = jnp.float32
 bf16 = jnp.bfloat16
 
@@ -20,10 +19,11 @@
 
 def kernel(
     rows_n, feat_n, scale,
-    features, weight, bias, out_grad, keys, inverse_root,
+    features_hbm, weight_hbm, out_grad_hbm, neighbours_hbm, bias, counts, block_cols,
     hidden, input_grad, weight_grad, bias_grad,
     window, adj, adj_t, features_t, part_out, part_in, own, grad_proj,
     wsend, wrecv, zbuf, bsend, brecv, bz,
+    features, weight, out_grad, neighbours, keys, inverse_root, load_sem,
     fwd_send, fwd_recv, bwd_send, bwd_recv, ws_sem, wr_sem, zs_sem, zr_sem,
     bs_sem, br_sem, bzs_sem, bzr_sem,
 ):
@@ -103,6 +103,24 @@
     each(rows_n, lambda d: greet(row_peer(d)))
     each(feat_n, lambda d: greet(feat_peer(d)))
 
+    loads = [
+        pltpu.make_async_copy(src, dst, load_sem.at[i])
+        for i, (src, dst) in enumerate(
+            (
+                (features_hbm, features),
+                (weight_hbm, weight),
+                (neighbours_hbm, neighbours),
+                (out_grad_hbm, out_grad),
+            )
+        )
+    ]
+    for load in loads:
+        load.start()
+    root_row = lax.rsqrt(1.0 + counts[...].astype(f32))
+    inverse_root[...] = jnp.broadcast_to(root_row, (LANES, n)).T
+    loads[0].wait()
+    loads[1].wait()
+
     for c in range(chunks):
         product = matmul(features[...], weight[:, cols(c)])
         window[c, pl.ds(n, n), :] = (product * inverse_root[...]).astype(bf16)
@@ -112,21 +130,36 @@
         fwd(1, c).start()
 
     features_t[...] = features[...].T
-    columns = lax.broadcasted_iota(jnp.int32, (GROUP, 3 * n), 1)
-
-    def fill(g, carry):
-        at = pl.ds(pl.multiple_of(g * GROUP, GROUP), GROUP)
-        mine = keys[at, :]
-        total = jnp.zeros((GROUP, 3 * n), jnp.int32)
-        for k in range(keys.shape[1]):
-            total = total + (mine[:, k : k + 1] == columns).astype(jnp.int32)
-        adj[at, :] = total.astype(f32).astype(bf16)
-        return carry
-
-    lax.fori_loop(0, n // GROUP, fill, 0)
+    loads[2].wait()
+    tile_count, slot_count = block_cols.shape
+    all_tiles = tile_count * count
+    slots = neighbours.shape[0]
+    slot_ids = lax.broadcasted_iota(jnp.int32, (slots, LANES), 0)
+    row_ids = lax.broadcasted_iota(jnp.int32, (LANES, LANES), 0)
+    for t in range(tile_count):
+        named = neighbours[:, cols(t)] // LANES
+        place = neighbours[:, cols(t)] - named * LANES
+        base = jnp.zeros_like(named)
+        for s in range(slot_count):
+            tile = lax.rem(block_cols[t, s] - (me - 1) * tile_count + all_tiles, all_tiles)
+            base = jnp.where(named == s, tile, base)
+        used = slot_ids < counts[:, cols(t)]
+        keys[:, cols(t)] = jnp.where(used, base * LANES + place, -1)
+
+        def fill(j, carry):
+            start = pl.multiple_of(j * LANES, LANES)
+            mine = keys[:, cols(t)] - start
+            total = jnp.zeros((LANES, LANES), jnp.int32)
+            for k in range(slots):
+                total = total + (mine[k : k + 1, :] == row_ids).astype(jnp.int32)
+            adj_t[pl.ds(start, LANES), cols(t)] = total.astype(f32).astype(bf16)
+            return carry
+
+        lax.fori_loop(0, 3 * n // LANES, fill, 0)
     for j in range(3):
         at = pl.ds(j * n, n)
-        adj_t[at, :] = adj[:, at].T
+        adj[:, at] = adj_t[at, :].T
+    loads[3].wait()
 
     bsend[...] = jnp.zeros_like(bsend)
     for c in range(chunks):
@@ -201,8 +234,6 @@
 
 def local(features, weight, layer_bias, block_cols, neighbours, row_counts, out_grad):
     n, width = features.shape
-    tile_count, slot_count = block_cols.shape
-    tile_rows = n // tile_count
     slots = neighbours.shape[1]
     rows_n, feat_n = lax.axis_size("rows"), lax.axis_size("feat")
     devices = rows_n * feat_n
@@ -210,17 +241,8 @@
     chunks = width // LANES
     share = width // rows_n
 
-    window_start = (lax.axis_index(("rows", "feat")) - 1) * tile_count
-    local_slot = jnp.mod(block_cols - window_start, tile_count * devices)
-    used = jnp.arange(slots, dtype=jnp.int32)[None, :] < row_counts[:, None]
-    named = neighbours // tile_rows
-    base = jnp.zeros_like(neighbours)
-    for s in range(slot_count):
-        base = jnp.where(named == s, jnp.repeat(local_slot[:, s], tile_rows)[:, None], base)
-    keys = jnp.where(used, base * tile_rows + neighbours % tile_rows, -1)
-    inverse_root = lax.rsqrt(1.0 + row_counts.astype(f32))[:, None]
-
     vmem = pl.BlockSpec(memory_space=pltpu.VMEM)
+    anywhere = pl.BlockSpec(memory_space=pltpu.HBM)
     bias_rows = max(8, chunks)
     dma = pltpu.SemaphoreType.DMA
     hidden, input_grad, weight_grad, bias_grad = pl.pallas_call(
@@ -231,7 +253,7 @@
             jax.ShapeDtypeStruct((share, width), f32),
             jax.ShapeDtypeStruct((bias_rows, LANES), f32),
         ),
-        in_specs=[vmem] * 6,
+        in_specs=[anywhere] * 4 + [vmem] * 2 + [pl.BlockSpec(memory_space=pltpu.SMEM)],
         out_specs=(vmem,) * 4,
         scratch_shapes=[
             pltpu.VMEM((chunks, 3 * n, LANES), bf16),
@@ -248,18 +270,25 @@
             pltpu.VMEM((bias_rows, LANES), f32),
             pltpu.VMEM((rows_n, bias_rows, LANES), f32),
             pltpu.VMEM((feat_n, bias_rows, LANES), f32),
+            pltpu.VMEM((n, width), bf16),
+            pltpu.VMEM((width, width), bf16),
+            pltpu.VMEM((n, width), bf16),
+            pltpu.VMEM((slots, n), jnp.int32),
+            pltpu.VMEM((slots, n), jnp.int32),
+            pltpu.VMEM((n, LANES), f32),
+            dma((4,)),
             dma((2, chunks)), dma((2, chunks)), dma((2, chunks)), dma((2, chunks)),
             dma((chunks, rows_n)), dma((chunks, rows_n)),
             dma((chunks, feat_n)), dma((chunks, feat_n)),
             dma((rows_n,)), dma((rows_n,)), dma((feat_n,)), dma((feat_n,)),
         ],
         compiler_params=pltpu.CompilerParams(
-            collective_id=0, has_side_effects=True, vmem_limit_bytes=48 * 2**20
+            collective_id=0, has_side_effects=True, vmem_limit_bytes=63 * 2**20
         ),
         cost_estimate=pl.CostEstimate(
             flops=18 * n * width * width, bytes_accessed=12 * n * width, transcendentals=n * width
         ),
-    )(features, weight, layer_bias[None, :], out_grad, keys, inverse_root)
+    )(features, weight, out_grad, neighbours.T, layer_bias[None, :], row_counts[None, :], block_cols)
     part_bias = lax.dynamic_slice_in_dim(
         bias_grad.reshape(-1), lax.axis_index("rows") * share, share, 0
     )

time: 70.4 us -> 69.7 us (0.990)
  Pallas kernels: 62 us -> 64 us
  local copies, waits for them, and re-layouts: 6.69 us -> 4.88 us
    pallas_call x1, Pallas kernels: 62 us -> 64 us  [local(): pl.pallas_call(functools.partial(kernel, rows_n, feat_n, scale), out_shap...]
    unnamed x18 -> x7, local copies, waits for them, and re-layouts: 5.49 us -> 3.61 us
where the time goes in v2:
time: 69.7 us; the launch traced here: 69.5 us
  Pallas kernels  64 us (92%)
  local copies, waits for them, and re-layouts  4.88 us (7%)
    pallas_call x1, Pallas kernels, local(): pl.pallas_call(functools.partial(kernel, rows_n, feat_n, scale), out_shap...  64 us
    unnamed x7, local copies, waits for them, and re-layouts  3.61 us

profile of v2, /device:TPU:0, one launch (start us, length us, event | category | flops | bytes accessed | tf_op | source)
XLA Modules:
  0.0 69.5 jit_solution(2012346489853681870)
XLA Ops:
  0.6 64.0 %shard_map.102 = (bf16[512,512]{1,0:T(8,128)(2,1)}, bf16[512,512]{1,0:T(8,128)(2,1)}, f32[64,512]{1,0:T(8,128)}, f32[8,128]{1,0:T(8,128)}) custom-call(bf16[512,512]{1,0:T(8,128)(2,1)} %features_hbm.1, bf16[512,512]{1,0:T(8,128)(2,1)} %weight_hbm.1, bf16[512,512]{1,0:T(8,128)(2,1)} %out_grad_hbm.1, s32[30,512]{1,0:T(8,128)} %bitcast.4, f32[1,512]{1,0:T(1,128)} %bitcast.5, ...), custom_call_target="tpu_custom_call" | custom-call | flops 2415919104 | bytes 3145728 | tf_op jit(solution)/shard_map/pallas_call | solution.py:248
  64.6 1.3 %dynamic_slice.3 = f32[64]{0:T(128)} dynamic-slice(f32[1024]{0:T(1024)} %bitcast.7, s32[]{:T(128)S(6)} %select_n.3), dynamic_slice_sizes={64} | dynamic-slice | bytes 516 | tf_op jit(solution)/shard_map/dynamic_slice | solution.py:292
  65.9 0.0 copy-start
  65.9 1.9 %copy.14 = bf16[512,512]{1,0:T(8,128)(2,1)} copy(bf16[512,512]{1,0:T(8,128)(2,1)} %get-tuple-element.16) | data formatting | bytes 1048576
  67.8 0.0 copy-done
  67.8 0.0 copy-start.1
  67.8 0.8 %copy.15 = bf16[512,512]{1,0:T(8,128)(2,1)} copy(bf16[512,512]{1,0:T(8,128)(2,1)S(1)} %copy-done) | data formatting | bytes 1048576
  68.6 0.2 copy-done.1
  68.8 0.7 copy.16
Async XLA Ops:
  65.9 1.9 %copy-start = (bf16[512,512]{1,0:T(8,128)(2,1)S(1)}, bf16[512,512]{1,0:T(8,128)(2,1)}, u32[]{:S(2)}) copy-start(bf16[512,512]{1,0:T(8,128)(2,1)} %get-tuple-element.17) | copy-start | bytes 1572868
  67.8 1.0 %copy-start.1 = (f32[64,512]{1,0:T(8,128)S(1)}, f32[64,512]{1,0:T(8,128)}, u32[]{:S(2)}) copy-start(f32[64,512]{1,0:T(8,128)} %get-tuple-element.18) | copy-start | bytes 393220

commit v3 on v2

--- a/solution.py
+++ b/solution.py
@@ -283,7 +283,7 @@
             dma((rows_n,)), dma((rows_n,)), dma((feat_n,)), dma((feat_n,)),
         ],
         compiler_params=pltpu.CompilerParams(
-            collective_id=0, has_side_effects=True, vmem_limit_bytes=63 * 2**20
+            collective_id=0, has_side_effects=True, vmem_limit_bytes=48 * 2**20
         ),
         cost_estimate=pl.CostEstimate(
             flops=18 * n * width * width, bytes_accessed=12 * n * width, transcendentals=n * width

time: 69.7 us -> 71.2 us (1.022)
  local copies, waits for them, and re-layouts: 4.88 us -> 7.48 us
  Pallas kernels: 64 us -> 62.7 us
    unnamed x7 -> x17, local copies, waits for them, and re-layouts: 3.61 us -> 6.89 us
    pallas_call x1, Pallas kernels: 64 us -> 62.7 us  [local(): pl.pallas_call(functools.partial(kernel, rows_n, feat_n, scale), out_shap...]
where the time goes in v3:
time: 71.2 us; the launch traced here: 70.8 us
  Pallas kernels  62.7 us (88%)
  local copies, waits for them, and re-layouts  7.48 us (11%)
    pallas_call x1, Pallas kernels, local(): pl.pallas_call(functools.partial(kernel, rows_n, feat_n, scale), out_shap...  62.7 us
    unnamed x17, local copies, waits for them, and re-layouts  6.89 us

profile of v3, /device:TPU:0, one launch (start us, length us, event | category | flops | bytes accessed | tf_op | source)
XLA Modules:
  0.0 70.8 jit_solution(3114018517351545417)
XLA Ops:
  0.6 0.0 copy-start.6
  0.6 0.0 copy-start.5
  0.7 0.0 copy-start.4
  0.7 0.7 copy-done.6
  1.3 0.0 copy-done.5
  1.3 0.0 copy-done.4
  1.4 0.0 copy-start
  1.4 1.0 %copy-done = bf16[512,512]{1,0:T(8,128)(2,1)S(1)} copy-done((bf16[512,512]{1,0:T(8,128)(2,1)S(1)}, bf16[512,512]{1,0:T(8,128)(2,1)}, u32[]{:S(2)}) %copy-start) | copy-done | bytes 524312
  2.4 0.0 copy-start.1
  2.4 1.0 %copy-done.1 = bf16[512,512]{1,0:T(8,128)(2,1)S(1)} copy-done((bf16[512,512]{1,0:T(8,128)(2,1)S(1)}, bf16[512,512]{1,0:T(8,128)(2,1)}, u32[]{:S(2)}) %copy-start.1) | copy-done | bytes 524312
  3.4 0.0 copy-start.2
  3.4 1.0 %copy-done.2 = bf16[512,512]{1,0:T(8,128)(2,1)S(1)} copy-done((bf16[512,512]{1,0:T(8,128)(2,1)S(1)}, bf16[512,512]{1,0:T(8,128)(2,1)}, u32[]{:S(2)}) %copy-start.2) | copy-done | bytes 524312
  4.5 0.0 copy-start.3
  4.5 0.8 %copy-done.3 = s32[512,30]{0,1:T(8,128)S(1)} copy-done((s32[512,30]{0,1:T(8,128)S(1)}, s32[512,30]{0,1:T(8,128)}, u32[]{:S(2)}) %copy-start.3) | copy-done | bytes 61464
  5.3 62.7 %shard_map.102 = (bf16[512,512]{1,0:T(8,128)(2,1)S(1)}, bf16[512,512]{1,0:T(8,128)(2,1)S(1)}, f32[64,512]{1,0:T(8,128)S(1)}, f32[8,128]{1,0:T(8,128)S(1)}) custom-call(bf16[512,512]{1,0:T(8,128)(2,1)S(1)} %copy-done, bf16[512,512]{1,0:T(8,128)(2,1)S(1)} %copy-done.1, bf16[512,512]{1,0:T(8,128)(2,1)S(1)} %copy-done.2, s32[30,512]{1,0:T(8,128)S(1)} %bitcast.4, ...), custom_call_target="tpu_custom_call" | custom-call | flops 2415919104 | bytes 3145728 | tf_op jit(solution)/shard_map/pallas_call | solution.py:248
  68.0 0.6 dynamic_slice.3
  68.6 0.8 %copy.14 = bf16[512,512]{1,0:T(8,128)(2,1)} copy(bf16[512,512]{1,0:T(8,128)(2,1)S(1)} %get-tuple-element.16) | data formatting | bytes 1048576
  69.4 0.8 %copy.15 = bf16[512,512]{1,0:T(8,128)(2,1)} copy(bf16[512,512]{1,0:T(8,128)(2,1)S(1)} %get-tuple-element.17) | data formatting | bytes 1048576
  70.2 0.7 copy.16
Async XLA Ops:
  0.6 0.7 copy-start.6
  0.6 0.7 copy-start.5
  0.7 0.7 copy-start.4
  1.4 1.0 %copy-start = (bf16[512,512]{1,0:T(8,128)(2,1)S(1)}, bf16[512,512]{1,0:T(8,128)(2,1)}, u32[]{:S(2)}) copy-start(bf16[512,512]{1,0:T(8,128)(2,1)} %features_hbm.1) | copy-start | bytes 1572868
  2.4 1.0 %copy-start.1 = (bf16[512,512]{1,0:T(8,128)(2,1)S(1)}, bf16[512,512]{1,0:T(8,128)(2,1)}, u32[]{:S(2)}) copy-start(bf16[512,512]{1,0:T(8,128)(2,1)} %weight_hbm.1) | copy-start | bytes 1572868
  3.4 1.0 %copy-start.2 = (bf16[512,512]{1,0:T(8,128)(2,1)S(1)}, bf16[512,512]{1,0:T(8,128)(2,1)}, u32[]{:S(2)}) copy-start(bf16[512,512]{1,0:T(8,128)(2,1)} %out_grad_hbm.1) | copy-start | bytes 1572868
  4.5 0.8 %copy-start.3 = (s32[512,30]{0,1:T(8,128)S(1)}, s32[512,30]{0,1:T(8,128)}, u32[]{:S(2)}) copy-start(s32[512,30]{0,1:T(8,128)} %param.11) | copy-start | bytes 184324
